TPU v7x, 256 devices: a whole 4x4x8 slice. The times are simulated.
256 devices in a mesh: lon: 8 (over z_lo, core), lat: 32 (over y, z_hi, x).
Axes of the slice: x: 4, y: 4, z: 8 (z_hi: 2, z_lo: 4; z = z_hi * 4 + z_lo), core: 2. Of those that a mesh axis runs over, the one named last changes fastest.
Arguments:
- east_adjoint: float32 [8, 2048, 2048], P(None, 'lat', 'lon'), may hold values from -6 to 6
- north_adjoint: float32 [8, 2048, 2048], P(None, 'lat', 'lon'), may hold values from -6 to 6
- height_adjoint: float32 [8, 2048, 2048], P(None, 'lat', 'lon'), may hold values from -6 to 6
- zonal_courant: float32 [8, 2048], P(None, 'lat'), may hold values from -0.4 to 0.4
- meridional_courant: float32 [8, 2048], P(None, 'lat'), may hold values from -0.4 to 0.4
- vertical_inverse: float32 [8, 8], replicated, may hold values from -2 to 2
- pass_counts: int32 [512], replicated, may hold values from 1 to 16, as said below
Outputs:
- east_result: float32 [8, 2048, 2048], P(None, 'lat', 'lon')
- north_result: float32 [8, 2048, 2048], P(None, 'lat', 'lon')
- height_result: float32 [8, 2048, 2048], P(None, 'lat', 'lon')
Inputs may be any that keep to these rules, and one draw needn't show every extreme that they name: `pass_counts`: the rows next to the two poles (entries 0 and 511) have exactly 16 passes; every row of both bands has at least one.
All inputs are finite; a program needn't handle non-finite values.
Results may differ from a plain program's by a relative error of at most 0.00007.
Values sent between devices are 32-bit elements; how exact they have to be, the bound alone decides.
No kernel may reach another device: no remote copies, remote signals or barrier semaphores. Data moves between devices by JAX's collectives and lax.ppermute only.
A program may use at most 64 MiB of HBM per device.

v0:
```python
import jax
import jax.numpy as jnp
from jax import lax
from jax.experimental import pallas as pl
from jax.experimental.pallas import tpu as pltpu
from jax.sharding import PartitionSpec as P

MAXP = 16
REACH = 3
WIDE = MAXP + REACH
LANES = 128
SPAN = 3 * LANES
SHARE = 33

gravity_weight = 0.3
divergence_weight = 0.3

VMEM = pl.BlockSpec(memory_space=pltpu.VMEM)
SMEM = pl.BlockSpec(memory_space=pltpu.SMEM)
HBM = pl.BlockSpec(memory_space=pltpu.HBM)

EDGE_SLOTS = ((0, 0), (0, 1), (1, 0), (1, 1), (1, 2), (2, 0), (2, 1))


HEIGHTS = 8 * WIDE + 4
EDGES = 8 * WIDE + 88
PAYLOAD = EDGES + 24


def lanes():
    return lax.broadcasted_iota(jnp.int32, (8, LANES), 1)


def turn(values, steps):
    return pltpu.roll(values, steps % values.shape[-1], values.ndim - 1)


def zonal(values):
    return turn(values, -1) - turn(values, 1)


def is_even(axis):
    return lax.rem(lax.axis_index(axis), 2) == 0


def row_count(counts_ref, row, rows, lat_blocks):
    band = counts_ref.shape[0] // 2
    blocks = band // rows
    position = lax.axis_index("lat")
    north = position < blocks
    south = position >= lat_blocks - blocks
    place = jnp.where(north, position, jnp.where(south, position - lat_blocks + 2 * blocks, 0))
    return jnp.where(north | south, counts_ref[place * rows + row], 0)


def undo(count):
    power = jnp.left_shift(1, MAXP - count).astype(jnp.float32)
    return power * power * (2.0 ** (-2 * MAXP))


class Stream:
    GROUPS = (1, 1, 2, 4, 8)

    def __init__(self, masks):
        self.masks = masks

    def start(self):
        zero = jnp.zeros((8, LANES), jnp.float32)
        return [zero] * (2 * MAXP + sum(self.GROUPS))

    def step(self, state, tile):
        state = list(state)
        at, later = 0, 2 * MAXP
        for mask, size in zip(self.masks, self.GROUPS):
            entered = tile
            for _ in range(size):
                half = state[at] + tile
                state[at], tile = tile, state[at + 1] + half
                state[at + 1] = half
                at += 2
            delayed = state[later]
            state[later : later + size] = state[later + 1 : later + size] + [entered]
            later += size
            tile = jnp.where(mask, tile, delayed)
        return state, tile


def group_masks(count):
    rest = count - 1
    bits = [jnp.bitwise_and(jnp.right_shift(rest, b), 1) == 1 for b in range(4)]
    used = count > 0
    return [used] + [used & bit for bit in bits]


def pack_kernel(
    e_hbm, n_hbm, h_hbm, a_ref, b_ref, wind_ref, height_ref, edge_ref, x_ref, t_ref, sems
):
    copies = []
    for f, ref in enumerate((e_hbm, n_hbm, h_hbm)):
        for t in range(2):
            copy = pltpu.make_async_copy(
                ref.at[:, :, pl.ds(LANES * t, LANES)],
                x_ref.at[f, t].reshape(8, 64, LANES),
                sems.at[f, t],
            )
            copy.start()
            copies.append(copy)
    winds = wind_ref.reshape(256 * 8, LANES)
    for f in range(3):
        for t in range(2):
            copies[2 * f + t].wait()
            for q in range(4):
                turned = x_ref[f, t, pl.ds(LANES * q, LANES), :].T
                if f < 2:
                    winds[pl.ds(1024 * t + 4 * f + q, LANES, stride=8), :] = turned
                else:
                    height_ref[pl.ds(512 * t + q, LANES, stride=4), :] = turned
    for side in range(2):
        for slot, (field, distance) in enumerate(EDGE_SLOTS):
            row = 63 - distance if side else distance
            place = 8 * (len(EDGE_SLOTS) * side + slot)
            for t in range(2):
                t_ref[t, pl.ds(place, 8), :] = x_ref[field, t, pl.ds(row, 8, stride=64), :]
    for t in range(2):
        t_ref[t, pl.ds(112, 16), :] = jnp.zeros((16, LANES), jnp.float32)
        edge_ref[pl.ds(LANES * t, LANES), :] = t_ref[t].T
    even = is_even("lon")
    last = 256 - WIDE
    for ref, right in ((a_ref, even), (b_ref, jnp.logical_not(even))):
        first = jnp.where(right, last, 0)
        ref[pl.ds(0, 8 * WIDE), :] = wind_ref[pl.ds(first, WIDE)].reshape(8 * WIDE, LANES)
        ref[pl.ds(HEIGHTS, 4 * WIDE), :] = jnp.where(
            right, height_ref[pl.ds(4 * last, 4 * WIDE), :], height_ref[pl.ds(0, 4 * WIDE), :]
        )
        ref[pl.ds(EDGES, WIDE), :] = jnp.where(
            right, edge_ref[pl.ds(last, WIDE), :], edge_ref[pl.ds(0, WIDE), :]
        )


def edge_kernel(
    lat_blocks, band,
    turned_ref, rb_ref, ra_ref, count_ref, mer_ref, a_ref, b_ref, own_ref, z_ref, o_ref
):
    even_lon = is_even("lon")
    even_lat = is_even("lat")
    lane = lanes()
    halo = pl.ds(EDGES, WIDE)
    z_ref[pl.ds(24, 256), :] = turned_ref[...]
    z_ref[pl.ds(24 - WIDE, WIDE), :] = jnp.where(even_lon, rb_ref[halo, :], ra_ref[halo, :])
    z_ref[pl.ds(280, WIDE), :] = jnp.where(even_lon, ra_ref[halo, :], rb_ref[halo, :])
    z_ref[pl.ds(280 + WIDE, 5), :] = jnp.zeros((5, LANES), jnp.float32)
    polar = is_polar(lat_blocks, 64, band)

    @pl.when(jnp.logical_not(polar))
    def _():
        o_ref[...] = z_ref[pl.ds(24 - REACH, 8 * SHARE), :]

    @pl.when(polar)
    def _():
        count = count_ref[...]
        stream = Stream(group_masks(count))
        scale = undo(count)
        state = stream.start()
        for i in range(SHARE + 2 * MAXP):
            state, tile = stream.step(state, z_ref[pl.ds(24 - WIDE + i, 8, stride=SHARE), :])
            if i >= 2 * MAXP:
                o_ref[pl.ds(i - 2 * MAXP, 8, stride=SHARE), :] = tile * scale

    first = o_ref[pl.ds(REACH, LANES), :].T
    second = o_ref[pl.ds(REACH + LANES, LANES), :].T
    o_ref[pl.ds(REACH, REACH), :] = o_ref[pl.ds(REACH + 2 * LANES, REACH), :]
    third = o_ref[pl.ds(0, LANES), :].T
    packs = []
    for side in range(2):
        sense = -1.0 if side else 1.0

        def row(field, distance):
            slot = EDGE_SLOTS.index((field, distance))
            place = 8 * (len(EDGE_SLOTS) * side + slot)
            own = slice(place, place + 8)
            return jnp.concatenate([first[own], second[own], turn(third[own], -REACH)], axis=-1)

        e0, e1, n0, n1, n2, h0, h1 = (row(*slot) for slot in EDGE_SLOTS)
        outer = h0 + gravity_weight * (zonal(e0) + sense * n1)
        inner = h1 + gravity_weight * (zonal(e1) + sense * (n2 - n0))
        own_ref[side] = outer
        at = 63 if side else 0
        pack = jnp.broadcast_to(mer_ref[:, at : at + 1], (8, LANES))
        out = []
        for slot, value in enumerate((outer, inner, e0, n0)):
            out += [value[:, :LANES], value[:, LANES : 2 * LANES]]
            start = 2 * REACH * slot
            inside = (lane >= start) & (lane < start + 2 * REACH)
            pack = jnp.where(inside, turn(value[:, 2 * LANES :], REACH + start), pack)
        packs.append(out + [pack])
    for place, (top, bottom) in enumerate(zip(*packs)):
        a_ref[pl.ds(8 * place, 8)] = jnp.where(even_lat, bottom, top)
        b_ref[pl.ds(8 * place, 8)] = jnp.where(even_lat, top, bottom)


def following(rows):
    count = rows.shape[0]
    return pltpu.roll(rows, count - 1, 0) - pltpu.roll(rows, 1, 0)


def is_polar(lat_blocks, rows, band):
    position = lax.axis_index("lat")
    return (position < band // rows) | (position >= lat_blocks - band // rows)


def leaves_results(lat_blocks, rows, band):
    position = lax.axis_index("lat")
    return (position == band // rows - 1) | (position >= lat_blocks - band // rows)


def whole(f_ref, f, start, rows):
    tiles = range(f_ref.shape[1])
    return jnp.concatenate([f_ref[f, t, pl.ds(start, rows), :] for t in tiles], axis=-1)


def new_heights(f_ref, v_ref):
    tiles = f_ref.shape[1]

    def weight(k, l):
        return jnp.concatenate([v_ref[k, l]] * tiles, axis=-1)

    for first in range(0, 64, 8):
        old = []
        for l in range(8):
            start = 64 * l + first
            north = whole(f_ref, 1, start, 8)
            above = whole(f_ref, 1, start - 1, 8) if start else pltpu.roll(north, 1, 0)
            below = whole(f_ref, 1, start + 1, 8) if start < 512 - 8 else pltpu.roll(north, 7, 0)
            slope = zonal(whole(f_ref, 0, start, 8)) + (below - above)
            old.append(whole(f_ref, 2, start, 8) + gravity_weight * slope)
        for l in range(8):
            total = weight(0, l) * old[0]
            for k in range(1, 8):
                total = total + weight(k, l) * old[k]
            for t in range(tiles):
                place = pl.ds(64 * l + first, 8)
                f_ref[2, t, place, :] = total[:, LANES * t : LANES * (t + 1)]


def results(f_ref, zb_ref, mb_ref, write):
    tiles = f_ref.shape[1]
    for l in range(8):
        h2 = whole(f_ref, 2, 64 * l, 64)
        h2_zonal = zonal(h2)
        e1 = whole(f_ref, 0, 64 * l, 64) + divergence_weight * h2_zonal
        n1 = whole(f_ref, 1, 64 * l, 64) + divergence_weight * following(h2)
        zon = jnp.concatenate([zb_ref[l]] * tiles, axis=-1)
        mer = jnp.concatenate([mb_ref[l]] * tiles, axis=-1)
        for f, field in enumerate((e1, n1, h2)):
            slope = h2_zonal if f == 2 else zonal(field)
            write(f, l, field + zon * slope + following(mer * field))


def edge_row(side, distance):
    return 63 - distance if side else distance


def inner_results(f_ref, zb_ref, mb_ref, ob_ref):
    def write(f, l, value):
        for t in range(2):
            ob_ref[f, t, pl.ds(64 * l, 64), :] = value[:, LANES * t : LANES * (t + 1)]

    results(f_ref, zb_ref, mb_ref, write)


def interior_kernel(
    lat_blocks,
    _, wind_ref, height_ref, counts_ref, zon_ref, mer_ref, v_ref,
    f_ref, ob_ref, edge_ref, zb_ref, mb_ref, count_ref, edge_count_ref, vb_ref, vc_ref,
    wo_ref, ho_ref,
):
    lane = lanes()
    level = lax.broadcasted_iota(jnp.int32, (8, LANES), 0)
    polar = is_polar(lat_blocks, 64, counts_ref.shape[0] // 2)

    @pl.when(polar)
    def _():
        count = jnp.zeros((8, LANES), jnp.int32)
        for row in range(64):
            value = row_count(counts_ref, row, 64, lat_blocks)
            count = jnp.where(jnp.bitwise_and(lane, 63) == row, value, count)
        count_ref[...] = count
        count = jnp.zeros((8, LANES), jnp.int32)
        for side in range(2):
            for slot, (_, distance) in enumerate(EDGE_SLOTS):
                value = row_count(counts_ref, edge_row(side, distance), 64, lat_blocks)
                place = 8 * (len(EDGE_SLOTS) * side + slot)
                count = jnp.where(lane >= place, value, count)
        edge_count_ref[...] = count

    @pl.when(jnp.logical_not(polar))
    def _():
        count_ref[...] = jnp.zeros((8, LANES), jnp.int32)
        edge_count_ref[...] = jnp.zeros((8, LANES), jnp.int32)

    @pl.when(polar)
    def _():
        count = count_ref[...]
        stream = Stream(group_masks(count))
        scale = undo(count)

        def winds(chunk, state):
            for u in range(8):
                i = 8 * chunk + u
                state, tile = stream.step(state, wind_ref[i])
                wo_ref[i] = tile * scale
            return tuple(state)

        lax.fori_loop(0, 32, winds, tuple(stream.start()))

        def heights(chunk, state):
            for u in range(0, 8, 2):
                i = 8 * chunk + u
                low = height_ref[pl.ds(pl.multiple_of(4 * i, 8), 8), :]
                high = height_ref[pl.ds(pl.multiple_of(4 * i + 448, 8), 8), :]
                pair = jnp.where(level < 4, low, pltpu.roll(high, 4, 0))
                state, tile = stream.step(state, pair)
                ho_ref[i] = tile * scale
                pair = jnp.where(level < 4, pltpu.roll(low, 4, 0), high)
                state, tile = stream.step(state, pair)
                ho_ref[i + 1] = tile * scale
            return tuple(state)

        lax.fori_loop(0, 18, heights, tuple(stream.start()))
        wo = wo_ref.reshape(wo_ref.shape[0] * 8, LANES)
        ho = ho_ref.reshape(ho_ref.shape[0] * 8, LANES)
        for f in range(3):
            for q in range(4):
                for t in range(2):
                    if f < 2:
                        tall = wo[pl.ds(8 * (MAXP + LANES * t) + 4 * f + q, LANES, stride=8), :]
                    else:
                        tall = ho[pl.ds(8 * MAXP * (1 + t) + q + 4 * t, LANES, stride=8), :]
                    f_ref[f, t, pl.ds(LANES * q, LANES), :] = tall.T

    def keep_edge(slot, field, distance):
        for side in range(2):
            for t in range(2):
                place = pl.ds(edge_row(side, distance), 8, stride=64)
                edge_ref[side, slot, :, pl.ds(LANES * t, LANES)] = f_ref[field, t, place, :]

    for d in range(4):
        keep_edge(d, 0, d)
        keep_edge(4 + d, 1, d)
    for k in range(8):
        for l in range(8):
            vb_ref[k, l] = jnp.full((8, LANES), v_ref[k, l], jnp.float32)
    for k, column in enumerate(mixing(v_ref)):
        vc_ref[k] = column
    for l in range(8):
        zb_ref[l] = jnp.broadcast_to(zon_ref[l : l + 1, :], (LANES, 64)).T
        mb_ref[l] = jnp.broadcast_to(mer_ref[l : l + 1, :], (LANES, 64)).T

    new_heights(f_ref, vb_ref)
    for d in range(1, 5):
        keep_edge(7 + d, 2, d)

    @pl.when(jnp.logical_not(leaves_results(lat_blocks, 64, counts_ref.shape[0] // 2)))
    def _():
        inner_results(f_ref, zb_ref, mb_ref, ob_ref)


SIDE = 64
OWN = SIDE - WIDE


def fix_kernel(
    lat_blocks, band,
    _, inner_f_ref, inner_ref, wind_ref, height_ref, rb_ref, ra_ref, zb_ref, mb_ref, count_ref, v_ref,
    ob_ref, all_ref, edge_ref,
    f_ref, wz_ref, hz_ref,
):
    even_lon = is_even("lon")
    level = lax.broadcasted_iota(jnp.int32, (8, LANES), 0)
    polar = is_polar(lat_blocks, 64, band)

    @pl.when(leaves_results(lat_blocks, 64, band))
    def _():
        inner_results(inner_f_ref, zb_ref, mb_ref, ob_ref)

    def left(place):
        return jnp.where(even_lon, rb_ref[place, :], ra_ref[place, :])

    def right(place):
        return jnp.where(even_lon, ra_ref[place, :], rb_ref[place, :])

    for i in range(WIDE):
        wz_ref[MAXP + i] = left(pl.ds(8 * i, 8))
        wz_ref[MAXP + SIDE + OWN + i] = right(pl.ds(8 * i, 8))
    wz_ref[pl.ds(MAXP + WIDE, OWN)] = wind_ref[pl.ds(0, OWN)]
    wz_ref[pl.ds(MAXP + SIDE, OWN)] = wind_ref[pl.ds(256 - OWN, OWN)]
    for i in range(SIDE):
        if i < WIDE:
            low = left(pl.ds(HEIGHTS + 4 * i, 8))
        else:
            low = height_ref[pl.ds(4 * (i - WIDE), 8), :]
        if i < OWN:
            high = height_ref[pl.ds(4 * (256 - OWN + i) - 4, 8), :]
        else:
            high = right(pl.ds(HEIGHTS + 4 * (i - OWN) - 4, 8))
        hz_ref[MAXP + i] = jnp.where(level < 4, low, high)

    @pl.when(polar)
    def _():
        count = count_ref[...]
        stream = Stream(group_masks(count))
        scale = undo(count)

        def run(ref, base):
            def steps(chunk, state):
                for u in range(8):
                    i = base + 8 * chunk + u
                    state, tile = stream.step(state, ref[MAXP + i])
                    ref[i] = tile * scale
                return tuple(state)

            lax.fori_loop(0, SIDE // 8, steps, tuple(stream.start()))

        run(wz_ref, 0)
        run(wz_ref, SIDE)
        run(hz_ref, 0)

    wz = wz_ref.reshape(wz_ref.shape[0] * 8, LANES)
    hz = hz_ref.reshape(hz_ref.shape[0] * 8, LANES)
    for f in range(3):
        for q in range(4):
            if f < 2:
                tall = wz[pl.ds(8 * MAXP + 4 * f + q, LANES, stride=8), :]
            else:
                parts = [hz[pl.ds(8 * MAXP + q + 4 * s, SIDE, stride=8), :] for s in range(2)]
                tall = jnp.concatenate(parts, axis=0)
            f_ref[f, 0, pl.ds(LANES * q, LANES), :] = tall.T

    lane = lanes()

    def keep_edge(slot, field, distance):
        for side in range(2):
            near = f_ref[field, 0, pl.ds(edge_row(side, distance), 8, stride=64), :]
            west, east = turn(near, -WIDE), turn(near, WIDE)
            first, second = inner_ref[side, slot, :, :LANES], inner_ref[side, slot, :, LANES:]
            edge_ref[side, slot, :, pl.ds(0, LANES)] = jnp.where(lane < 24, west, first)
            edge_ref[side, slot, :, pl.ds(LANES, LANES)] = jnp.where(lane >= 104, east, second)
            edge_ref[side, slot, :, pl.ds(2 * LANES, LANES)] = jnp.where(lane < 64, east, west)

    for d in range(4):
        keep_edge(d, 0, d)
        keep_edge(4 + d, 1, d)

    new_heights(f_ref, v_ref)
    for d in range(1, 5):
        keep_edge(7 + d, 2, d)
    wide_lane = lax.broadcasted_iota(jnp.int32, (64, LANES), 1)

    def write(f, l, near):
        west, east = turn(near, -WIDE), turn(near, WIDE)
        rows = pl.ds(64 * l, 64)
        all_ref[f, 0, rows, :] = jnp.where(wide_lane < 22, west, ob_ref[f, 0, rows, :])
        all_ref[f, 1, rows, :] = jnp.where(wide_lane >= 106, east, ob_ref[f, 1, rows, :])

    results(f_ref, zb_ref, mb_ref, write)


def mixing(v_ref):
    level = lax.broadcasted_iota(jnp.int32, (8, LANES), 0)
    columns = []
    for k in range(8):
        column = jnp.full((8, LANES), v_ref[k, 0], jnp.float32)
        for l in range(1, 8):
            column = jnp.where(level == l, v_ref[k, l], column)
        columns.append(column)
    return columns


def mix(columns, height):
    tiles = []
    for t in range(height.shape[-1] // LANES):
        tile = height[..., t * LANES : (t + 1) * LANES]
        total = None
        for k, column in enumerate(columns):
            term = column * jnp.broadcast_to(tile[..., k : k + 1, :], tile.shape)
            total = term if total is None else total + term
        tiles.append(total)
    return jnp.concatenate(tiles, axis=-1)


def wide(column):
    return jnp.concatenate([column] * (SPAN // LANES), axis=-1)


def finish_kernel(
    lat_blocks,
    edge_ref, own_ref, all_ref, gb_ref, ga_ref, zon_ref, mer_ref, v_ref,
    oe_ref, on_ref, oh_ref,
    ob_ref, sems, edge_sems,
):
    outs = (oe_ref, on_ref, oh_ref)
    copies = []
    for f, out in enumerate(outs):
        for t in range(2):
            copy = pltpu.make_async_copy(
                all_ref.at[f, t].reshape(8, 64, LANES).at[:, pl.ds(8, 48)],
                out.at[:, pl.ds(8, 48), pl.ds(LANES * t, LANES)],
                sems.at[f, t],
            )
            copy.start()
            copies.append(copy)
    position = lax.axis_index("lat")
    even_lat = is_even("lat")
    lane = lanes()
    columns = [v_ref[k] for k in range(8)]
    for side in range(2):
        top = side == 0
        sense = 1.0 if top else -1.0
        pole = position == (0 if top else lat_blocks - 1)
        turned = jnp.where(pole, -1.0, 1.0)

        def ghost_tile(place):
            a, b = ga_ref[pl.ds(8 * place, 8)], gb_ref[pl.ds(8 * place, 8)]
            return jnp.where(even_lat, b, a) if top else jnp.where(even_lat, a, b)

        pack = ghost_tile(8)

        def ghost(slot):
            third = turn(pack, -REACH - 2 * REACH * slot)
            return jnp.concatenate([ghost_tile(2 * slot), ghost_tile(2 * slot + 1), third], axis=-1)

        e = {d: edge_ref[side, d] for d in range(4)}
        n = {d: edge_ref[side, 4 + d] for d in range(4)}
        h2 = {d: edge_ref[side, 7 + d] for d in range(1, 5)}
        e[-1] = ghost(2)
        n[-1] = ghost(3) * turned
        h2[-2] = mix(columns, ghost(1))
        h2[-1] = mix(columns, ghost(0) + (gravity_weight * sense) * n[0])
        h2[0] = mix(columns, own_ref[side] - (gravity_weight * sense) * n[-1])
        e1, n1, h2_zonal = {}, {}, {}
        for d in range(-1, 4):
            h2_zonal[d] = zonal(h2[d])
            e1[d] = e[d] + divergence_weight * h2_zonal[d]
            n1[d] = n[d] + (divergence_weight * sense) * (h2[d + 1] - h2[d - 1])
        mer_ghost = wide(jnp.where(lane < LANES // 2, turn(pack, LANES // 2), pack))

        def coefficient(ref, d):
            row = edge_row(side, d)
            return wide(jnp.broadcast_to(ref[:, row : row + 1], (8, LANES)))

        zon = {d: coefficient(zon_ref, d) for d in range(3)}
        mer = {d: coefficient(mer_ref, d) for d in range(4)}
        for f, field in enumerate((e1, n1, h2)):
            mer[-1] = mer_ghost if f == 0 else mer_ghost * turned
            flow = {d: mer[d] * field[d] for d in range(-1, 4)}
            for t in range(2):
                for l in range(8):
                    ob_ref[f, side, t, pl.ds(8 * l, 8), :] = all_ref[
                        f, t, pl.ds(64 * l + 56 * side, 8), :
                    ]
            for d in range(3 if f == 1 else 2):
                slope = h2_zonal[d] if f == 2 else zonal(field[d])
                value = field[d] + zon[d] * slope + sense * (flow[d + 1] - flow[d - 1])
                for t in range(2):
                    ob_ref[f, side, t, pl.ds(d if top else 7 - d, 8, stride=8), :] = value[
                        :, LANES * t : LANES * (t + 1)
                    ]
    for side in range(2):
        for f, out in enumerate(outs):
            for t in range(2):
                copy = pltpu.make_async_copy(
                    ob_ref.at[f, side, t].reshape(8, 8, LANES),
                    out.at[:, pl.ds(56 * side, 8), pl.ds(LANES * t, LANES)],
                    edge_sems.at[f, side, t],
                )
                copy.start()
                copies.append(copy)
    for copy in copies:
        copy.wait()


def body(
    lat_blocks, lon_blocks, axes,
    east_adjoint, north_adjoint, height_adjoint,
    zonal_courant, meridional_courant, vertical_inverse, pass_counts,
):
    f32 = jnp.float32
    fields = tuple(
        pltpu.with_memory_space_constraint(x, pltpu.HBM)
        for x in (east_adjoint, north_adjoint, height_adjoint)
    )

    def in_vmem(*dims):
        return pltpu.VMEM(dims, f32)

    def params():
        return pltpu.CompilerParams(vmem_limit_bytes=40 * 1024 * 1024)

    lon_a, lon_b, winds, heights, edge_rows, local = pl.pallas_call(
        pack_kernel,
        out_shape=(
            in_vmem(PAYLOAD, LANES), in_vmem(PAYLOAD, LANES),
            in_vmem(256, 8, LANES), in_vmem(1024, LANES), in_vmem(256, LANES),
            in_vmem(3, 2, 512, LANES),
        ),
        in_specs=[HBM] * 3,
        out_specs=(VMEM,) * 6,
        scratch_shapes=[pltpu.VMEM((2, LANES, LANES), f32), pltpu.SemaphoreType.DMA((3, 2))],
        compiler_params=params(),
        name="pack",
    )(*fields)

    def other_lon(o):
        return (((o + 1) ^ 1) - 1) % lon_blocks

    recv_a = lax.ppermute(lon_a, "lon", [(o, o ^ 1) for o in range(lon_blocks)])
    recv_b = lax.ppermute(lon_b, "lon", [(o, other_lon(o)) for o in range(lon_blocks)])

    by_row = in_vmem(8, 64, LANES)
    by_count = pltpu.VMEM((8, LANES), jnp.int32)
    inner_f, inner, inner_edges, zon_wide, mer_wide, counts, edge_counts, weights, columns = pl.pallas_call(
        lambda *refs: interior_kernel(lat_blocks, *refs),
        out_shape=(
            in_vmem(3, 2, 512, LANES), in_vmem(3, 2, 512, LANES), in_vmem(2, 12, 8, 256),
            by_row, by_row, by_count, by_count, in_vmem(8, 8, 8, LANES), in_vmem(8, 8, LANES),
        ),
        in_specs=[VMEM] * 3 + [SMEM, VMEM, VMEM, SMEM],
        out_specs=(VMEM,) * 9,
        input_output_aliases={0: 0},
        scratch_shapes=[
            pltpu.VMEM((272, 8, LANES), f32),
            pltpu.VMEM((160, 8, LANES), f32),
        ],
        compiler_params=params(),
        cost_estimate=pl.CostEstimate(flops=100000000, bytes_accessed=20000000, transcendentals=0),
        name="interior",
    )(
        local, winds, heights, pass_counts, zonal_courant, meridional_courant, vertical_inverse
    )

    band = pass_counts.shape[0] // 2
    lat_a, lat_b, own_edges = pl.pallas_call(
        lambda *refs: edge_kernel(lat_blocks, band, *refs),
        out_shape=(in_vmem(72, LANES), in_vmem(72, LANES), in_vmem(2, 8, SPAN)),
        in_specs=[VMEM] * 5,
        out_specs=(VMEM,) * 3,
        scratch_shapes=[pltpu.VMEM((304, LANES), f32), pltpu.VMEM((264, LANES), f32)],
        compiler_params=params(),
        name="edge",
    )(edge_rows, recv_b, recv_a, edge_counts, meridional_courant)

    def index(a, o):
        return o * lat_blocks + a if axes[0] == "lon" else a * lon_blocks + o

    def other_lat(a, o):
        if a in (0, lat_blocks - 1):
            return a, (o + lon_blocks // 2) % lon_blocks
        return ((a + 1) ^ 1) - 1, o

    pairs = [
        (index(a, o), index(*other_lat(a, o))) for a in range(lat_blocks) for o in range(lon_blocks)
    ]
    ghost_a = lax.ppermute(lat_a, "lat", [(a, a ^ 1) for a in range(lat_blocks)])
    ghost_b = lax.ppermute(lat_b, axes, pairs)

    block = jax.ShapeDtypeStruct(east_adjoint.shape, f32)
    _, final, edges = pl.pallas_call(
        lambda *refs: fix_kernel(lat_blocks, band, *refs),
        out_shape=(
            in_vmem(3, 2, 512, LANES), in_vmem(3, 2, 512, LANES), in_vmem(2, 12, 8, SPAN)
        ),
        in_specs=[VMEM] * 11,
        out_specs=(VMEM,) * 3,
        input_output_aliases={0: 0},
        scratch_shapes=[
            pltpu.VMEM((3, 1, 512, LANES), f32),
            pltpu.VMEM((MAXP + 2 * SIDE, 8, LANES), f32),
            pltpu.VMEM((MAXP + SIDE, 8, LANES), f32),
        ],
        compiler_params=params(),
        cost_estimate=pl.CostEstimate(flops=50000000, bytes_accessed=10000000, transcendentals=0),
        name="fix",
    )(
        inner, inner_f, inner_edges, winds, heights, recv_b, recv_a, zon_wide, mer_wide, counts, weights,
    )

    return pl.pallas_call(
        lambda *refs: finish_kernel(lat_blocks, *refs),
        out_shape=(block,) * 3,
        in_specs=[VMEM] * 8,
        out_specs=(HBM,) * 3,
        scratch_shapes=[
            pltpu.VMEM((3, 2, 2, 64, LANES), f32),
            pltpu.SemaphoreType.DMA((3, 2)),
            pltpu.SemaphoreType.DMA((3, 2, 2)),
        ],
        compiler_params=params(),
        name="finish",
    )(
        edges, own_edges, final, ghost_b, ghost_a, zonal_courant, meridional_courant, columns
    )


def solution(mesh):
    sizes = dict(mesh.shape)
    axes = tuple(mesh.axis_names)
    spread_out = P(None, "lat", "lon")
    return jax.shard_map(
        lambda *args: body(sizes["lat"], sizes["lon"], axes, *args),
        mesh=mesh,
        in_specs=(spread_out,) * 3 + (P(None, "lat"), P(None, "lat"), P(), P()),
        out_specs=(spread_out,) * 3,
        check_vma=False,
    )
```

profile of v0, /device:TPU:24, one launch (start us, length us, event | category | flops | bytes accessed | tf_op | source)
XLA Modules:
  0.0 24.7 jit_solution(6144634152763943839)
XLA Ops:
  0.6 0.0 copy-start
  0.6 0.0 copy-start.1
  0.7 0.0 copy-start.3
  0.7 0.0 copy-start.2
  0.7 1.9 %pack.1 = (f32[264,128]{1,0:T(8,128)S(1)}, f32[264,128]{1,0:T(8,128)S(1)}, f32[256,8,128]{2,1,0:T(8,128)S(1)}, f32[1024,128]{1,0:T(8,128)S(1)}, f32[256,128]{1,0:T(8,128)S(1)}, /*index=5*/f32[3,2,512,128]{3,2,1,0:T(8,128)S(1)}) custom-call(f32[8,64,256]{2,1,0:T(8,128)} %e_hbm.1, f32[8,64,256]{2,1,0:T(8,128)} %n_hbm.1, f32[8,64,256]{2,1,0:T(8,128)} %h_hbm.1), custom_call_target="tpu_custom_call" | custom-call | tf_op jit(solution)/shard_map/pack/pallas_call | solution.py:599
  2.6 4.2 %collective-permute-start = (f32[264,128]{1,0:T(8,128)S(1)}, f32[264,128]{1,0:T(8,128)S(1)}, u32[]{:S(2)}, u32[]{:S(2)}) collective-permute-start(f32[264,128]{1,0:T(8,128)S(1)} %get-tuple-element.29), channel_id=1, source_target_pairs={{0,224},{32,64},{64,32},{96,128},{128,96},{160,192},{192,160},{224... | collective-permute-start | bytes 405512 | tf_op jit(solution)/shard_map/ppermute | solution.py:617
  6.7 0.0 collective-permute-start.1
  6.7 0.0 copy-done
  6.7 0.0 copy-done.1
  6.7 0.0 copy-done.3
  6.7 0.0 copy-done.2
  6.8 3.1 %interior.1 = (f32[3,2,512,128]{3,2,1,0:T(8,128)S(1)}, f32[3,2,512,128]{3,2,1,0:T(8,128)S(1)}, f32[2,12,8,256]{3,2,1,0:T(8,128)S(1)}, f32[8,64,128]{2,1,0:T(8,12...) custom-call(f32[3,2,512,128]{3,2,1,0:T(8,128)S(1)} %get-tuple-elemen, ...), custom_call_target="tpu_custom_call", output_to_operand_aliasing={{0}: (0, {})} | custom-call | flops 100000000 | bytes 20000000 | tf_op jit(solution)/shard_map/interior/pallas_call | solution.py:621
  9.8 0.2 collective-permute-done.refs_5_.refs_1_
  10.0 0.0 collective-permute-done.1.refs_6_.refs_2_
  10.0 0.4 %edge.1 = (f32[72,128]{1,0:T(8,128)S(1)}, f32[72,128]{1,0:T(8,128)S(1)}, f32[2,8,384]{2,1,0:T(8,128)S(1)}) custom-call(f32[256,128]{1,0:T(8,128)S(1)} %get-tuple-element.36.refs_0_, f32[264,128]{1,0:T(8,128)S(1)} %collective-permute-done.refs_5_.refs_1_, f32[264,128]{1,0:T(8,128)S(1)} %collective-permute-done.1.refs_6_.refs_2_, ...), custom_call_target="tpu_custom_call" | custom-call | tf_op jit(solution)/shard_map/edge/pallas_call | solution.py:642
  10.4 9.1 %collective-permute-start.2 = (f32[72,128]{1,0:T(8,128)S(1)}, f32[72,128]{1,0:T(8,128)S(1)}, u32[]{:S(2)}, u32[]{:S(2)}) collective-permute-start(f32[72,128]{1,0:T(8,128)S(1)} %get-tuple-element.40), channel_id=1, source_target_pairs={{0,128},{32,160},{64,192},{96,224},{128,0},{160,32},{192,64},{224,... | collective-permute-start | bytes 110600 | tf_op jit(solution)/shard_map/ppermute | solution.py:664
  19.5 0.0 collective-permute-start.3
  19.5 2.9 %fix.1 = (f32[3,2,512,128]{3,2,1,0:T(8,128)S(1)}, f32[3,2,512,128]{3,2,1,0:T(8,128)S(1)}, f32[2,12,8,384]{3,2,1,0:T(8,128)S(1)}) custom-call(f32[3,2,512,128]{3,2,1,0:T(8,128)S(1)} %get-tuple-element.26.refs_0_, f32[3,2,512,128]{3,2,1,0:T(8,128)S(1)} %get-tuple-element.27.refs_1_, ...), custom_call_target="tpu_custom_call", output_to_operand_aliasing={{0}: (0, {})} | custom-call | flops 50000000 | bytes 10000000 | tf_op jit(solution)/shard_map/fix/pallas_call | solution.py:667
  22.4 0.0 collective-permute-done.2.refs_3_
  22.5 1.0 %collective-permute-done.3.refs_4_ = f32[72,128]{1,0:T(8,128)S(1)} collective-permute-done((f32[72,128]{1,0:T(8,128)S(1)}, f32[72,128]{1,0:T(8,128)S(1)}, u32[]{:S(2)}, u32[]{:S(2)}) %collective-permute-start.3) | collective-permute-done | bytes 36896 | tf_op jit(solution)/shard_map/ppermute | solution.py:663
  23.4 1.3 %finish.1 = (f32[8,64,256]{2,1,0:T(8,128)}, f32[8,64,256]{2,1,0:T(8,128)}, f32[8,64,256]{2,1,0:T(8,128)}) custom-call(f32[2,12,8,384]{3,2,1,0:T(8,128)S(1)} %get-tuple-element.35.refs_0_, f32[2,8,384]{2,1,0:T(8,128)S(1)} %get-tuple-element.38.refs_1_, f32[3,2,512,128]{3,2,1,0:T(8,128)S(1)} %get-tuple-element.39.refs_2_, ...), custom_call_target="tpu_custom_call" | custom-call | tf_op jit(solution)/shard_map/finish/pallas_call | solution.py:687
Async XLA Ops:
  0.6 6.1 %copy-start = (f32[8,64]{1,0:T(8,128)S(1)}, f32[8,64]{1,0:T(8,128)}, u32[]{:S(2)}) copy-start(f32[8,64]{1,0:T(8,128)} %refs_6_.3) | copy-start | bytes 6148
  0.6 6.1 %copy-start.1 = (f32[8,64]{1,0:T(8,128)S(1)}, f32[8,64]{1,0:T(8,128)}, u32[]{:S(2)}) copy-start(f32[8,64]{1,0:T(8,128)} %refs_5_.3) | copy-start | bytes 6148
  0.7 6.1 %copy-start.3 = (s32[512]{0:T(512)S(1)}, s32[512]{0:T(512)}, u32[]{:S(2)}) copy-start(s32[512]{0:T(512)} %refs_3_.1) | copy-start | bytes 6148
  0.7 6.1 %copy-start.2 = (f32[8,8]{1,0:T(8,128)S(1)}, f32[8,8]{1,0:T(8,128)}, u32[]{:S(2)}) copy-start(f32[8,8]{1,0:T(8,128)} %refs_6_.2) | copy-start | bytes 772
  2.6 7.5 %collective-permute-start = (f32[264,128]{1,0:T(8,128)S(1)}, f32[264,128]{1,0:T(8,128)S(1)}, u32[]{:S(2)}, u32[]{:S(2)}) collective-permute-start(f32[264,128]{1,0:T(8,128)S(1)} %get-tuple-element.29), channel_id=1, source_target_pairs={{0,224},{32,64},{64,32},{96,128},{128,96},{160,192},{192,160},{224... | collective-permute-start | bytes 405512 | tf_op jit(solution)/shard_map/ppermute | solution.py:617
  6.7 3.3 %collective-permute-start.1 = (f32[264,128]{1,0:T(8,128)S(1)}, f32[264,128]{1,0:T(8,128)S(1)}, u32[]{:S(2)}, u32[]{:S(2)}) collective-permute-start(f32[264,128]{1,0:T(8,128)S(1)} %get-tuple-element.30), channel_id=1, source_target_pairs={{0,32},{32,0},{64,96},{96,64},{128,160},{160,128},{192,224},{224,1... | collective-permute-start | bytes 405512 | tf_op jit(solution)/shard_map/ppermute | solution.py:616
  10.4 12.0 %collective-permute-start.2 = (f32[72,128]{1,0:T(8,128)S(1)}, f32[72,128]{1,0:T(8,128)S(1)}, u32[]{:S(2)}, u32[]{:S(2)}) collective-permute-start(f32[72,128]{1,0:T(8,128)S(1)} %get-tuple-element.40), channel_id=1, source_target_pairs={{0,128},{32,160},{64,192},{96,224},{128,0},{160,32},{192,64},{224,... | collective-permute-start | bytes 110600 | tf_op jit(solution)/shard_map/ppermute | solution.py:664
  19.5 4.0 %collective-permute-start.3 = (f32[72,128]{1,0:T(8,128)S(1)}, f32[72,128]{1,0:T(8,128)S(1)}, u32[]{:S(2)}, u32[]{:S(2)}) collective-permute-start(f32[72,128]{1,0:T(8,128)S(1)} %get-tuple-element.41), channel_id=1, source_target_pairs={{0,1},{1,0},{2,3},{3,2},{4,5},{5,4},{6,7},{7,6},{8,9},{9,8},{10,11... | collective-permute-start | bytes 110600 | tf_op jit(solution)/shard_map/ppermute | solution.py:663
where the time goes:
time: 24.8 us; the launch traced here: 24.7 us
  starting transfers between devices  13.2 us (53%)
  Pallas kernels  9.58 us (39%)
  waiting for transfers between devices  1.2 us (5%)
  between operations  0.72 us (3%)
    ppermute x1, starting transfers between devices, body(): ghost_b = lax.ppermute(lat_b, axes, pairs)  9.05 us
    ppermute x1, starting transfers between devices, body(): lax.ppermute(lon_b, 'lon', [(o, other_lon(o)) for o in range(lon_blocks)])  4.15 us
    pallas_call x1, Pallas kernels, body(): pl.pallas_call(lambda *refs: interior_kernel(lat_blocks, *refs), out_shap...  3.08 us
    pallas_call x1, Pallas kernels, body(): pl.pallas_call(lambda *refs: fix_kernel(lat_blocks, band, *refs), out_sha...  2.94 us
    pallas_call x1, Pallas kernels, body(): pl.pallas_call(pack_kernel, out_shape=(in_vmem(PAYLOAD, LANES), in_vmem(P...  1.89 us
    pallas_call x1, Pallas kernels, body(): pl.pallas_call(lambda *refs: finish_kernel(lat_blocks, *refs), out_shape=...  1.28 us
    ppermute x1, waiting for transfers between devices, body(): lax.ppermute(lat_a, 'lat', [(a, a ^ 1) for a in range(lat_blocks)])  0.99 us
  transfers between devices with their start and end apart: 4, of which 2 were waited for; matrix products, arithmetic and copies ran while one was open for 0% of the time, Pallas kernels for 24%

commit v1 on v0

--- a/solution.py
+++ b/solution.py
@@ -22,9 +22,9 @@
 EDGE_SLOTS = ((0, 0), (0, 1), (1, 0), (1, 1), (1, 2), (2, 0), (2, 1))
 
 
-HEIGHTS = 8 * WIDE + 4
-EDGES = 8 * WIDE + 88
-PAYLOAD = EDGES + 24
+HEIGHTS = 8 * WIDE
+EDGES = 12 * WIDE
+PAYLOAD = 248
 
 
 def lanes():

time: 24.8 us -> 24.6 us (level)
  transfers between devices with their start and end apart: 4 -> 4, of which waited for: 2 -> 1; matrix products, arithmetic and copies ran while one was open for 0% -> 0% of each run, Pallas kernels for 24% -> 25%
where the time goes in v1:
time: 24.6 us; the launch traced here: 24.5 us
  starting transfers between devices  13.2 us (54%)
  Pallas kernels  9.57 us (39%)
  waiting for transfers between devices  1.03 us (4%)
  between operations  0.72 us (3%)
    ppermute x1, starting transfers between devices, body(): ghost_b = lax.ppermute(lat_b, axes, pairs)  9.05 us
    ppermute x1, starting transfers between devices, body(): lax.ppermute(lon_b, 'lon', [(o, other_lon(o)) for o in range(lon_blocks)])  4.15 us
    pallas_call x1, Pallas kernels, body(): pl.pallas_call(lambda *refs: interior_kernel(lat_blocks, *refs), out_shap...  3.07 us
    pallas_call x1, Pallas kernels, body(): pl.pallas_call(lambda *refs: fix_kernel(lat_blocks, band, *refs), out_sha...  2.95 us
    pallas_call x1, Pallas kernels, body(): pl.pallas_call(pack_kernel, out_shape=(in_vmem(PAYLOAD, LANES), in_vmem(P...  1.89 us
    pallas_call x1, Pallas kernels, body(): pl.pallas_call(lambda *refs: finish_kernel(lat_blocks, *refs), out_shape=...  1.28 us
    ppermute x1, waiting for transfers between devices, body(): lax.ppermute(lat_a, 'lat', [(a, a ^ 1) for a in range(lat_blocks)])  0.99 us
  transfers between devices with their start and end apart: 4, of which 1 were waited for; matrix products, arithmetic and copies ran while one was open for 0% of the time, Pallas kernels for 25%

profile of v1, /device:TPU:24, one launch (start us, length us, event | category | flops | bytes accessed | tf_op | source)
XLA Modules:
  0.0 24.5 jit_solution(15512563785608703196)
XLA Ops:
  0.6 0.0 copy-start
  0.6 0.0 copy-start.1
  0.7 0.0 copy-start.3
  0.7 0.0 copy-start.2
  0.7 1.9 %pack.1 = (f32[248,128]{1,0:T(8,128)S(1)}, f32[248,128]{1,0:T(8,128)S(1)}, f32[256,8,128]{2,1,0:T(8,128)S(1)}, f32[1024,128]{1,0:T(8,128)S(1)}, f32[256,128]{1,0:T(8,128)S(1)}, /*index=5*/f32[3,2,512,128]{3,2,1,0:T(8,128)S(1)}) custom-call(f32[8,64,256]{2,1,0:T(8,128)} %e_hbm.1, f32[8,64,256]{2,1,0:T(8,128)} %n_hbm.1, f32[8,64,256]{2,1,0:T(8,128)} %h_hbm.1), custom_call_target="tpu_custom_call" | custom-call | tf_op jit(solution)/shard_map/pack/pallas_call | solution.py:599
  2.6 4.2 %collective-permute-start = (f32[248,128]{1,0:T(8,128)S(1)}, f32[248,128]{1,0:T(8,128)S(1)}, u32[]{:S(2)}, u32[]{:S(2)}) collective-permute-start(f32[248,128]{1,0:T(8,128)S(1)} %get-tuple-element.29), channel_id=1, source_target_pairs={{0,224},{32,64},{64,32},{96,128},{128,96},{160,192},{192,160},{224... | collective-permute-start | bytes 380936 | tf_op jit(solution)/shard_map/ppermute | solution.py:617
  6.7 0.0 collective-permute-start.1
  6.7 0.0 copy-done
  6.7 0.0 copy-done.1
  6.7 0.0 copy-done.3
  6.7 0.0 copy-done.2
  6.8 3.1 %interior.1 = (f32[3,2,512,128]{3,2,1,0:T(8,128)S(1)}, f32[3,2,512,128]{3,2,1,0:T(8,128)S(1)}, f32[2,12,8,256]{3,2,1,0:T(8,128)S(1)}, f32[8,64,128]{2,1,0:T(8,12...) custom-call(f32[3,2,512,128]{3,2,1,0:T(8,128)S(1)} %get-tuple-elemen, ...), custom_call_target="tpu_custom_call", output_to_operand_aliasing={{0}: (0, {})} | custom-call | flops 100000000 | bytes 20000000 | tf_op jit(solution)/shard_map/interior/pallas_call | solution.py:621
  9.8 0.0 collective-permute-done.refs_5_.refs_1_
  9.9 0.0 collective-permute-done.1.refs_6_.refs_2_
  9.9 0.4 %edge.1 = (f32[72,128]{1,0:T(8,128)S(1)}, f32[72,128]{1,0:T(8,128)S(1)}, f32[2,8,384]{2,1,0:T(8,128)S(1)}) custom-call(f32[256,128]{1,0:T(8,128)S(1)} %get-tuple-element.36.refs_0_, f32[248,128]{1,0:T(8,128)S(1)} %collective-permute-done.refs_5_.refs_1_, f32[248,128]{1,0:T(8,128)S(1)} %collective-permute-done.1.refs_6_.refs_2_, ...), custom_call_target="tpu_custom_call" | custom-call | tf_op jit(solution)/shard_map/edge/pallas_call | solution.py:642
  10.3 9.1 %collective-permute-start.2 = (f32[72,128]{1,0:T(8,128)S(1)}, f32[72,128]{1,0:T(8,128)S(1)}, u32[]{:S(2)}, u32[]{:S(2)}) collective-permute-start(f32[72,128]{1,0:T(8,128)S(1)} %get-tuple-element.40), channel_id=1, source_target_pairs={{0,128},{32,160},{64,192},{96,224},{128,0},{160,32},{192,64},{224,... | collective-permute-start | bytes 110600 | tf_op jit(solution)/shard_map/ppermute | solution.py:664
  19.3 0.0 collective-permute-start.3
  19.3 2.9 %fix.1 = (f32[3,2,512,128]{3,2,1,0:T(8,128)S(1)}, f32[3,2,512,128]{3,2,1,0:T(8,128)S(1)}, f32[2,12,8,384]{3,2,1,0:T(8,128)S(1)}) custom-call(f32[3,2,512,128]{3,2,1,0:T(8,128)S(1)} %get-tuple-element.26.refs_0_, f32[3,2,512,128]{3,2,1,0:T(8,128)S(1)} %get-tuple-element.27.refs_1_, ...), custom_call_target="tpu_custom_call", output_to_operand_aliasing={{0}: (0, {})} | custom-call | flops 50000000 | bytes 10000000 | tf_op jit(solution)/shard_map/fix/pallas_call | solution.py:667
  22.3 0.0 collective-permute-done.2.refs_3_
  22.3 1.0 %collective-permute-done.3.refs_4_ = f32[72,128]{1,0:T(8,128)S(1)} collective-permute-done((f32[72,128]{1,0:T(8,128)S(1)}, f32[72,128]{1,0:T(8,128)S(1)}, u32[]{:S(2)}, u32[]{:S(2)}) %collective-permute-start.3) | collective-permute-done | bytes 36896 | tf_op jit(solution)/shard_map/ppermute | solution.py:663
  23.3 1.3 %finish.1 = (f32[8,64,256]{2,1,0:T(8,128)}, f32[8,64,256]{2,1,0:T(8,128)}, f32[8,64,256]{2,1,0:T(8,128)}) custom-call(f32[2,12,8,384]{3,2,1,0:T(8,128)S(1)} %get-tuple-element.35.refs_0_, f32[2,8,384]{2,1,0:T(8,128)S(1)} %get-tuple-element.38.refs_1_, f32[3,2,512,128]{3,2,1,0:T(8,128)S(1)} %get-tuple-element.39.refs_2_, ...), custom_call_target="tpu_custom_call" | custom-call | tf_op jit(solution)/shard_map/finish/pallas_call | solution.py:687
Async XLA Ops:
  0.6 6.1 %copy-start = (f32[8,64]{1,0:T(8,128)S(1)}, f32[8,64]{1,0:T(8,128)}, u32[]{:S(2)}) copy-start(f32[8,64]{1,0:T(8,128)} %refs_6_.3) | copy-start | bytes 6148
  0.6 6.1 %copy-start.1 = (f32[8,64]{1,0:T(8,128)S(1)}, f32[8,64]{1,0:T(8,128)}, u32[]{:S(2)}) copy-start(f32[8,64]{1,0:T(8,128)} %refs_5_.3) | copy-start | bytes 6148
  0.7 6.1 %copy-start.3 = (s32[512]{0:T(512)S(1)}, s32[512]{0:T(512)}, u32[]{:S(2)}) copy-start(s32[512]{0:T(512)} %refs_3_.1) | copy-start | bytes 6148
  0.7 6.1 %copy-start.2 = (f32[8,8]{1,0:T(8,128)S(1)}, f32[8,8]{1,0:T(8,128)}, u32[]{:S(2)}) copy-start(f32[8,8]{1,0:T(8,128)} %refs_6_.2) | copy-start | bytes 772
  2.6 7.3 %collective-permute-start = (f32[248,128]{1,0:T(8,128)S(1)}, f32[248,128]{1,0:T(8,128)S(1)}, u32[]{:S(2)}, u32[]{:S(2)}) collective-permute-start(f32[248,128]{1,0:T(8,128)S(1)} %get-tuple-element.29), channel_id=1, source_target_pairs={{0,224},{32,64},{64,32},{96,128},{128,96},{160,192},{192,160},{224... | collective-permute-start | bytes 380936 | tf_op jit(solution)/shard_map/ppermute | solution.py:617
  6.7 3.1 %collective-permute-start.1 = (f32[248,128]{1,0:T(8,128)S(1)}, f32[248,128]{1,0:T(8,128)S(1)}, u32[]{:S(2)}, u32[]{:S(2)}) collective-permute-start(f32[248,128]{1,0:T(8,128)S(1)} %get-tuple-element.30), channel_id=1, source_target_pairs={{0,32},{32,0},{64,96},{96,64},{128,160},{160,128},{192,224},{224,1... | collective-permute-start | bytes 380936 | tf_op jit(solution)/shard_map/ppermute | solution.py:616
  10.3 12.0 %collective-permute-start.2 = (f32[72,128]{1,0:T(8,128)S(1)}, f32[72,128]{1,0:T(8,128)S(1)}, u32[]{:S(2)}, u32[]{:S(2)}) collective-permute-start(f32[72,128]{1,0:T(8,128)S(1)} %get-tuple-element.40), channel_id=1, source_target_pairs={{0,128},{32,160},{64,192},{96,224},{128,0},{160,32},{192,64},{224,... | collective-permute-start | bytes 110600 | tf_op jit(solution)/shard_map/ppermute | solution.py:664
  19.3 4.0 %collective-permute-start.3 = (f32[72,128]{1,0:T(8,128)S(1)}, f32[72,128]{1,0:T(8,128)S(1)}, u32[]{:S(2)}, u32[]{:S(2)}) collective-permute-start(f32[72,128]{1,0:T(8,128)S(1)} %get-tuple-element.41), channel_id=1, source_target_pairs={{0,1},{1,0},{2,3},{3,2},{4,5},{5,4},{6,7},{7,6},{8,9},{9,8},{10,11... | collective-permute-start | bytes 110600 | tf_op jit(solution)/shard_map/ppermute | solution.py:663
